TPU v7x, 768 devices: a whole 4x8x12 slice. The times are simulated.
768 devices in a mesh: tok: 16 (over x, y_lo), feat: 48 (over z, y_hi, core).
Axes of the slice: x: 4, y: 8 (y_hi: 2, y_lo: 4; y = y_hi * 4 + y_lo), z: 12, core: 2. Of those that a mesh axis runs over, the one named last changes fastest.
Arguments:
- source_acts: bfloat16 [3072, 4096], P('tok'), may hold values from -6 to 6
- target_acts: bfloat16 [3072, 4096], P('tok'), may hold values from -6 to 6
- enc_weight: bfloat16 [4096, 18432], P(None, 'feat'), may hold values from -0.09375 to 0.09375
- enc_bias: float32 [18432], P('feat'), may hold values from -1 to 1
- dec_weight: bfloat16 [18432, 4096], P('feat'), may hold values from -0.125 to 0.125
- active_blocks: int32 [48, 48], P('tok'), may hold values from 0 to 143, all different within a row
Outputs:
- grad_encoder: float32 [4096, 18432], P('tok', 'feat')
- grad_decoder: float32 [18432, 4096], P('feat', 'tok')
- recon_loss: float32 [], replicated
Inputs may be any that keep to these rules, and one draw needn't show every extreme that they name: `active_blocks`: each row lists 48 different blocks, and every block is listed by some row.
All inputs are finite; a program needn't handle non-finite values.
Results may differ from a plain program's by a relative error of at most 0.02.
Values may be sent and summed in bfloat16 or wider, within the bound.
A program may use at most 64 MiB of HBM per device.

v0:
```python
import jax
import jax.numpy as jnp
from jax import lax
from jax.sharding import PartitionSpec as P

BLOCK = 128
TILE = 64


def smooth_gate(values):
    return jax.nn.gelu(values, approximate=False)


def on_device(source_acts, target_acts, enc_weight, enc_bias, dec_weight, active_blocks):
    tok_rows, width = source_acts.shape
    feat_cols = enc_weight.shape[1]
    local_blocks = feat_cols // BLOCK
    first_block = lax.axis_index("feat") * local_blocks
    block_ids = first_block + jnp.arange(local_blocks, dtype=jnp.int32)
    tile_mask = jnp.any(active_blocks[:, :, None] == block_ids[None, None, :], axis=1).astype(
        jnp.float32
    )
    tile_count = tile_mask.shape[0]
    token_mask = jnp.broadcast_to(
        tile_mask[:, None, :, None], (tile_count, TILE, local_blocks, BLOCK)
    ).reshape(tok_rows, feat_cols)
    preact = (
        jnp.dot(source_acts, enc_weight, preferred_element_type=jnp.float32) + enc_bias[None, :]
    )
    gated, slope_fn = jax.vjp(smooth_gate, preact)
    features = (gated * token_mask).astype(jnp.bfloat16)
    partial_rec = jnp.dot(features, dec_weight, preferred_element_type=jnp.float32)
    total_rows = tok_rows * lax.axis_size("tok")
    recon = lax.psum(partial_rec, "feat")
    errors = recon - target_acts.astype(jnp.float32)
    recon_loss = lax.psum(jnp.sum(errors * errors), "tok") / (total_rows * width)
    errors_low = errors.astype(jnp.bfloat16)
    back_prop = lax.dot_general(
        errors_low, dec_weight, (((1,), (1,)), ((), ())), preferred_element_type=jnp.float32
    )
    grad_pre = (slope_fn(back_prop)[0] * token_mask).astype(jnp.bfloat16)
    enc_term = lax.dot_general(
        source_acts, grad_pre, (((0,), (0,)), ((), ())), preferred_element_type=jnp.float32
    )
    dec_term = lax.dot_general(
        features, errors_low, (((0,), (0,)), ((), ())), preferred_element_type=jnp.float32
    )
    grad_encoder, grad_decoder = (
        lax.psum_scatter(
            enc_term.astype(jnp.bfloat16), "tok", scatter_dimension=0, tiled=True
        ).astype(jnp.float32),
        lax.psum_scatter(
            dec_term.astype(jnp.bfloat16), "tok", scatter_dimension=1, tiled=True
        ).astype(jnp.float32),
    )
    return (grad_encoder, grad_decoder, recon_loss)


def solution(mesh):
    placed = (
        P("tok", None),
        P("tok", None),
        P(None, "feat"),
        P("feat"),
        P("feat", None),
        P("tok", None),
    )
    return jax.shard_map(
        on_device,
        mesh=mesh,
        in_specs=placed,
        out_specs=(P("tok", "feat"), P("feat", "tok"), P()),
        check_vma=False,
    )
```

profile of v0, /device:TPU:1, one launch (start us, length us, event | category | flops | bytes accessed | tf_op | source)
XLA Modules:
  0.0 756.2 jit_solution(4708270421249643429)
XLA Ops:
  7.2 0.0 copy-start
  7.2 0.0 all-reduce.2.cloned.1.call-start
  7.2 1.0 compare_reduce_fusion
  8.3 3.3 convolution_add_fusion
  11.6 0.0 copy-start.1
  11.7 0.1 broadcast_in_dim.2
  11.8 0.6 copy-done.1
  12.4 0.0 copy-done
  12.4 3.3 fusion.26
  15.6 0.0 all-reduce.2.cloned.1.call-update
  15.6 0.0 reduce-scatter.5.cloned.1.call-start
  15.7 531.5 %all-reduce.2.cloned.1.call-done = f32[192,4096]{1,0:T(8,128)} async-done(((f32[192,4096]{1,0:T(8,128)}), f32[192,4096]{1,0:T(8,128)}) %all-reduce.2.cloned.1.call-update) | async-done | bytes 3145744 | tf_op jit(solution)/shard_map/psum | solution.py:34
  547.2 5.8 convolution_convert_fusion
  553.0 0.0 reduce-scatter.5.cloned.1.call-update
  553.0 0.0 reduce-scatter.3.cloned.1.call-start
  553.0 7.5 fusion
  560.6 0.0 reduce-scatter.3.cloned.1.call-update
  560.6 3.8 multiply_reduce_fusion
  564.4 34.8 %psum.15 = f32[]{:T(128)} all-reduce(f32[]{:T(128)} %multiply_reduce_fusion), channel_id=1, replica_groups=mesh['tok'=16,'feat'=48] {'tok'}, use_global_device_ids=true, to_apply=%region_5.0 | all-reduce | flops 1 | bytes 8 | tf_op jit(solution)/shard_map/psum | solution.py:36
  599.8 44.2 %reduce-scatter.5.cloned.1.call-done = bf16[384,256]{1,0:T(8,128)(2,1)} async-done(((bf16[384,4096]{1,0:T(8,128)(2,1)}), bf16[384,256]{1,0:T(8,128)(2,1)}) %reduce-scatter.5.cloned.1.call-update) | async-done | bytes 196624 | tf_op jit(solution)/shard_map/reduce_scatter | solution.py:52
  644.1 1.7 convert_element_type.43
  645.8 101.0 %reduce-scatter.3.cloned.1.call-done = bf16[256,384]{0,1:T(8,128)(2,1)} async-done(((bf16[4096,384]{0,1:T(8,128)(2,1)}), bf16[256,384]{0,1:T(8,128)(2,1)}) %reduce-scatter.3.cloned.1.call-update) | async-done | bytes 196624 | tf_op jit(solution)/shard_map/reduce_scatter | solution.py:49
  746.7 1.8 copy.11
  (2 shorter events, 0.0 us)
Async XLA Ops:
  7.2 5.2 copy-start
  7.2 540.0 %all-reduce.2.cloned.1.call-start = ((), (), s32[]{:S(2)}) async-start(), calls=%async_computation.2 | async-start | bytes 6291456 | tf_op jit(solution)/shard_map/psum | solution.py:34
  11.6 0.7 copy-start.1
  15.6 628.4 %reduce-scatter.5.cloned.1.call-start = ((), (), s32[]{:S(2)}) async-start(), calls=%async_computation.4 | async-start | bytes 3342336 | tf_op jit(solution)/shard_map/reduce_scatter | solution.py:52
  553.0 193.8 %reduce-scatter.3.cloned.1.call-start = ((), (), s32[]{:S(2)}) async-start(), calls=%async_computation.3 | async-start | bytes 3342336 | tf_op jit(solution)/shard_map/reduce_scatter | solution.py:49
Sparse Core Ops, SparseCore 0:
  15.8 531.3 all-reduce.1
  553.1 90.9 reduce-scatter.4
  647.5 99.1 reduce-scatter.2
where the time goes:
time: 765 us; the launch traced here: 756 us
  waiting for transfers between devices  677 us (88%)
  blocking collectives  34.8 us (5%)
  matrix products  19.9 us (3%)
  between operations  15.6 us (2%)
    psum x1, waiting for transfers between devices, on_device(): recon = lax.psum(partial_rec, 'feat')  531 us
    reduce_scatter x1, waiting for transfers between devices, on_device(): lax.psum_scatter(enc_term.astype(jnp.bfloat16), 'tok', scatter_dimension=...  101 us
    reduce_scatter x1, waiting for transfers between devices, on_device(): lax.psum_scatter(dec_term.astype(jnp.bfloat16), 'tok', scatter_dimension=...  44.2 us
    psum x1, blocking collectives, on_device(): lax.psum(jnp.sum(errors * errors), 'tok') / (total_rows * width)  34.8 us
  transfers between devices with their start and end apart: 3, of which 3 were waited for; matrix products, arithmetic and copies ran while one was open for 2% of the time, Pallas kernels for 0%

commit v1 on v0

v1 whole, which is shorter than its diff:
```python
import functools
import math

import jax
import jax.numpy as jnp
from jax import lax
from jax.experimental import pallas as pl
from jax.experimental.pallas import tpu as pltpu
from jax.sharding import PartitionSpec as P

BLOCK = 128
TILE = 64
NX = 4
PER_Z = 4
MESH = pl.DeviceIdType.MESH
F32 = jnp.float32
BF16 = jnp.bfloat16


def remote(src, dst, send_sem, recv_sem, device):
    pltpu.make_async_remote_copy(
        src_ref=src, dst_ref=dst, send_sem=send_sem, recv_sem=recv_sem, device_id=device, device_id_type=MESH
    ).start()


def await_bytes(ref, sem):
    pltpu.make_async_copy(ref, ref, sem).wait()


def kernel(dims, src_hbm, tgt_hbm, enc_hbm, bias_ref, dec_hbm, act_ref, genc_ref, gdec_ref, loss_ref, *scratch):
    nt, ny, nz, rows, width, cols, ns = dims
    (src_v, enc_v, dec_v, tgt_v, acc, slope, srcd, fa, ga, err, errd, part, psend, precv, rsend, rrecv, ysend, yrecv, lbuf,
     load_sem, enc_sem, xs_sem, sf_sem, f_send, f_y, f_p, f_m, f_r, g_send, g_y, g_p, g_m, g_r, ps_send, ps_recv,
     rs_send, rs_recv, yh_send, yh_recv, e_zs, e_zp, e_zm, e_sib, d_xs, d_zs, d_zp, d_zm, d_sib, l_sem) = scratch
    half = width // 2
    dblk = width // nt
    chunk = rows // nz
    hrow = rows // 2
    sub_w = half // ns
    n_minus, n_plus = nz // 2, (nz - 1) // 2
    enc_parts = enc_sem.shape[0]
    kpart = width // enc_parts
    n_tiles = ps_recv.shape[0]
    tile_w = half // n_tiles

    t, f = lax.axis_index("tok"), lax.axis_index("feat")
    x, yl = t // ny, t % ny
    z, yh, c = f // PER_Z, (f // 2) % 2, f % 2

    def zmod(v):
        return lax.rem(v + nz, nz)

    def fid(zz, hh, cc):
        return (zz * 2 + hh) * 2 + cc

    def tid(xx, yy):
        return lax.rem(xx + NX, NX) * ny + lax.rem(yy + ny, ny)

    def rows_of(zz):
        return pl.ds(pl.multiple_of(zz * chunk, chunk), chunk)

    def dcols(tt):
        return pl.ds(pl.multiple_of(tt * dblk, dblk), dblk)

    z_up, z_down = (t, fid(zmod(z + 1), yh, c)), (t, fid(zmod(z - 1), yh, c))
    sibling, y_peer = (t, fid(z, yh, 1 - c)), (t, fid(z, 1 - yh, c))
    own_half = pl.ds(pl.multiple_of(hrow * c, hrow), hrow)
    sib_half = pl.ds(pl.multiple_of(hrow * (1 - c), hrow), hrow)
    my_cols = pl.ds(pl.multiple_of(half * c, half), half)
    my_groups = pl.ds(c * (nt // 2), nt // 2)

    def load_enc(k):
        part_rows = pl.ds(k * kpart, kpart)
        return pltpu.make_async_copy(enc_hbm.at[part_rows], enc_v.at[part_rows], enc_sem.at[k])

    loads = [
        pltpu.make_async_copy(src_hbm, src_v, load_sem.at[0]),
        pltpu.make_async_copy(dec_hbm, dec_v, load_sem.at[1]),
        pltpu.make_async_copy(tgt_hbm.at[rows_of(z), my_cols], tgt_v, load_sem.at[2]),
        pltpu.make_async_copy(src_hbm.at[own_half, dcols(t)], srcd.at[t, own_half], load_sem.at[3]),
    ]
    loads[0].start()
    for k in range(enc_parts):
        load_enc(k).start()
    for load in loads[1:]:
        load.start()

    barrier = pltpu.get_barrier_semaphore()
    for k in range(1, nt):
        pl.semaphore_signal(barrier, inc=1, device_id=(lax.rem(t + k, nt), f), device_id_type=MESH)
    for peer in (z_up, z_down, sibling, y_peer):
        pl.semaphore_signal(barrier, inc=1, device_id=peer, device_id_type=MESH)
    pl.semaphore_wait(barrier, nt - 1 + 4)

    for k in range(1, nt):
        to = lax.rem(t + k, nt)
        remote(src_hbm.at[own_half, dcols(to)], srcd.at[t, own_half], xs_sem.at[0], xs_sem.at[1], (to, f))

    loads[0].wait()
    acc[...] = jnp.broadcast_to(bias_ref[...], acc.shape)
    for k in range(enc_parts):
        load_enc(k).wait()
        part_rows = pl.ds(k * kpart, kpart)
        acc[...] += jnp.dot(src_v[:, part_rows], enc_v[part_rows, :], preferred_element_type=F32)

    for tile in range(rows // TILE):
        listed = act_ref[tile : tile + 1, :]
        for blk in range(cols // BLOCK):
            block_id = f * (cols // BLOCK) + blk
            active = jnp.max(jnp.where(listed == block_id, 1.0, 0.0), axis=1, keepdims=True)
            at = (pl.ds(tile * TILE, TILE), pl.ds(blk * BLOCK, BLOCK))
            v = acc[at]
            cdf = 0.5 * (1.0 + lax.erf(v * math.sqrt(0.5)))
            pdf = jnp.exp(-0.5 * v * v) * (1.0 / math.sqrt(2.0 * math.pi))
            fa[t, at[0], at[1]] = (v * cdf * active).astype(BF16)
            slope[at] = (cdf + v * pdf) * active

    def gather_start(buf, send, y_sem, p_sem, m_sem):
        for k in range(1, ny):
            remote(buf.at[t], buf.at[t], send, y_sem.at[k], (tid(x, yl + k), f))
        gather_x(buf, send, p_sem, m_sem, 0)

    def gather_x(buf, send, p_sem, m_sem, k):
        own = tid(x, yl - k)
        remote(buf.at[own], buf.at[own], send, p_sem.at[k], (tid(x + 1, yl), f))
        remote(buf.at[own], buf.at[own], send, m_sem.at[k], (tid(x - 1, yl), f))

    def gather_y(buf, send, y_sem, p_sem, m_sem, k):
        await_bytes(buf.at[tid(x, yl - k)], y_sem.at[k])
        gather_x(buf, send, p_sem, m_sem, k)

    def gather_relay(buf, send, p_sem, m_sem, r_sem, k):
        below, above = tid(x - 1, yl - k), tid(x + 1, yl - k)
        await_bytes(buf.at[below], p_sem.at[k])
        await_bytes(buf.at[above], m_sem.at[k])
        if k < ny // 2:
            remote(buf.at[below], buf.at[below], send, r_sem.at[k], (tid(x + 1, yl), f))
        else:
            remote(buf.at[above], buf.at[above], send, r_sem.at[k], (tid(x - 1, yl), f))

    def gather_far(buf, r_sem, k):
        await_bytes(buf.at[tid(x + 2, yl - k)], r_sem.at[k])

    gather_start(fa, f_send.at[0], f_y, f_p, f_m)

    loads[1].wait()

    @pl.loop(0, n_tiles)
    def _(n):
        at = pl.ds(pl.multiple_of(n * tile_w, tile_w), tile_w)
        full = pl.ds(pl.multiple_of(half * (1 - c) + n * tile_w, tile_w), tile_w)
        psend[:, at] = jnp.dot(fa[t], dec_v[:, full], preferred_element_type=F32).astype(BF16)
        remote(psend.at[:, at], precv.at[:, at], ps_send.at[0], ps_recv.at[n], sibling)

    @pl.loop(0, n_tiles)
    def _(n):
        at = pl.ds(pl.multiple_of(n * tile_w, tile_w), tile_w)
        full = pl.ds(pl.multiple_of(half * c + n * tile_w, tile_w), tile_w)
        part[:, at] = jnp.dot(fa[t], dec_v[:, full], preferred_element_type=F32)

    @pl.loop(0, n_tiles)
    def _(n):
        at = pl.ds(pl.multiple_of(n * tile_w, tile_w), tile_w)
        await_bytes(precv.at[:, at], ps_recv.at[n])
        part[:, at] += precv[:, at].astype(F32)

    def rs_step(slot, prev, owner, sub, device):
        value = part[rows_of(owner), pl.ds(sub * sub_w, sub_w)]
        if prev is not None:
            await_bytes(rrecv.at[prev, sub], rs_recv.at[prev, sub])
            value = value + rrecv[prev, sub].astype(F32)
        rsend[slot, sub] = value.astype(BF16)
        remote(rsend.at[slot, sub], rrecv.at[slot, sub], rs_send.at[0], rs_recv.at[slot, sub], device)

    for s in range(n_minus):
        for sub in range(ns):
            rs_step(s, s - 1 if s else None, zmod(z - (n_minus - s)), sub, z_down)
            if s < n_plus:
                rs_step(n_minus + s, n_minus + s - 1 if s else None, zmod(z + (n_plus - s)), sub, z_up)
    for sub in range(ns):
        value = part[rows_of(z), pl.ds(sub * sub_w, sub_w)]
        for last in (n_minus - 1, n_minus + n_plus - 1):
            await_bytes(rrecv.at[last, sub], rs_recv.at[last, sub])
            value = value + rrecv[last, sub].astype(F32)
        ysend[sub] = value.astype(BF16)
        remote(ysend.at[sub], yrecv.at[sub], yh_send.at[0], yh_recv.at[sub], y_peer)

    for sub in range(ns):
        await_bytes(yrecv.at[sub], yh_recv.at[sub])
        recon = ysend[sub].astype(F32) + yrecv[sub].astype(F32)
        target = tgt_v[:, pl.ds(sub * sub_w, sub_w)] if sub else None
        if sub == 0:
            loads[2].wait()
            target = tgt_v[:, pl.ds(0, sub_w)]
        at = pl.ds(pl.multiple_of(half * c + sub * sub_w, sub_w), sub_w)
        err[rows_of(z), at] = (recon - target.astype(F32)).astype(BF16)

    def ring_send(piece, send, p_sem, m_sem, up, down, own):
        if up is not None:
            remote(piece, piece, send, p_sem.at[up], z_up)
        if down is not None:
            remote(piece, piece, send, m_sem.at[down], z_down)
        remote(piece, piece, own[0], own[1], sibling)

    def ring(piece_of, send, p_sem, m_sem, sib_send, sib_own, sib_recv, between):
        ring_send(piece_of(z), send, p_sem, m_sem, 0, 0 if n_plus else None, (sib_send, sib_own))
        for s in range(1, n_minus + 1):
            piece = piece_of(zmod(z - s))
            await_bytes(piece, p_sem.at[s - 1])
            ring_send(piece, send, p_sem, m_sem, s if s < n_minus else None, None, (sib_send, sib_recv))
            if s <= n_plus:
                piece = piece_of(zmod(z + s))
                await_bytes(piece, m_sem.at[s - 1])
                ring_send(piece, send, p_sem, m_sem, None, s if s < n_plus else None, (sib_send, sib_recv))
            between(s)

    def err_piece(zz):
        return err.at[rows_of(zz), my_cols]

    mine = t // (nt // 2) == c

    def between_err(s):
        if s == 1:
            await_bytes(err_piece(z), e_sib.at[1])

            @pl.when(mine)
            def _():
                for k in range(1, nt):
                    to = lax.rem(t + k, nt)
                    remote(err.at[rows_of(z), dcols(to)], errd.at[t, z], d_xs.at[0], d_xs.at[1], (to, f))
                errd[t, z] = err[rows_of(z), dcols(t)]
        if s == 2:
            for k in range(1, ny):
                gather_y(fa, f_send.at[0], f_y, f_p, f_m, k)

    ring(err_piece, e_zs.at[0], e_zp, e_zm, e_sib.at[0], e_sib.at[1], e_sib.at[2], between_err)
    await_bytes(err.at[pl.ds(0, rows - chunk), pl.ds(0, half)], e_sib.at[2])

    acc[...] = jnp.zeros_like(acc)

    @pl.loop(0, enc_parts)
    def _(k):
        at = pl.ds(pl.multiple_of(k * kpart, kpart), kpart)
        acc[...] += lax.dot_general(err[:, at], dec_v[:, at], (((1,), (1,)), ((), ())), preferred_element_type=F32)

    ga[t] = (acc[...] * slope[...]).astype(BF16)
    gather_start(ga, g_send.at[0], g_y, g_p, g_m)

    total = jnp.zeros((16, 128), F32)
    for k in range(width // 128):
        piece = err[:, pl.ds(k * 128, 128)].astype(F32)
        piece = piece * piece
        for r in range(rows // 16):
            total = total + piece[r * 16 : (r + 1) * 16]
    lbuf[t] = total[:8] + total[8:]
    for k in range(1, nt):
        remote(lbuf.at[t], lbuf.at[t], l_sem.at[0], l_sem.at[1], (lax.rem(t + k, nt), f))

    def errd_piece(zz):
        return errd.at[my_groups, zz]

    @pl.when(mine)
    def _():
        await_bytes(errd.at[pl.ds(0, nt // 2 - 1), 0], d_xs.at[1])

    @pl.when(jnp.logical_not(mine))
    def _():
        await_bytes(errd.at[pl.ds(0, nt // 2), 0], d_xs.at[1])

    def between_errd(s):
        if s == 1:
            loads[3].wait()
            await_bytes(srcd.at[pl.ds(0, nt - 1), pl.ds(0, hrow)], xs_sem.at[1])
            remote(srcd.at[:, own_half], srcd.at[:, own_half], sf_sem.at[0], sf_sem.at[1], sibling)
            for k in range(ny):
                gather_relay(fa, f_send.at[0], f_p, f_m, f_r, k)
        if 2 <= s <= ny:
            gather_y(ga, g_send.at[0], g_y, g_p, g_m, s - 1)

    ring(errd_piece, d_zs.at[0], d_zp, d_zm, d_sib.at[0], d_sib.at[1], d_sib.at[1], between_errd)
    for k in range(n_minus + 1, ny + 1):
        between_errd(k)
    for k in range(ny):
        gather_relay(ga, g_send.at[0], g_p, g_m, g_r, k)
    for k in range(ny):
        gather_far(fa, f_r, k)
    await_bytes(errd.at[pl.ds(0, nt // 2)], d_sib.at[1])
    await_bytes(srcd.at[:, sib_half], sf_sem.at[1])

    across = (((0,), (0,)), ((), ()))
    gdec_ref[...] = jnp.zeros_like(gdec_ref)

    @pl.loop(0, nt)
    def _(g):
        gdec_ref[...] += lax.dot_general(fa[g], errd[g].reshape(rows, dblk), across, preferred_element_type=F32)

    genc_ref[...] = jnp.zeros_like(genc_ref)

    def enc_group(g):
        genc_ref[...] += lax.dot_general(srcd[g], ga[g], across, preferred_element_type=F32)

    @pl.loop(0, (NX - 1) * ny)
    def _(n):
        dx = n // ny
        enc_group(tid(x + jnp.where(dx == 2, NX - 1, dx), yl - n % ny))

    for k in range(ny):
        gather_far(ga, g_r, k)

    @pl.loop(0, ny)
    def _(k):
        enc_group(tid(x + 2, yl - k))

    await_bytes(lbuf.at[pl.ds(0, nt - 1)], l_sem.at[1])
    sums = lbuf[0]
    for k in range(1, nt):
        sums = sums + lbuf[k]
    loss_ref[0, 0] = jnp.sum(sums) / (rows * nt * width)

    await_bytes(srcd.at[pl.ds(0, nt - 1), pl.ds(0, hrow)], xs_sem.at[0])
    await_bytes(srcd.at[:, own_half], sf_sem.at[0])
    await_bytes(fa.at[pl.ds(0, nt - 1)], f_send.at[0])
    await_bytes(ga.at[pl.ds(0, nt - 1)], g_send.at[0])
    await_bytes(psend, ps_send.at[0])
    await_bytes(rsend, rs_send.at[0])
    await_bytes(ysend, yh_send.at[0])
    await_bytes(err.at[pl.ds(0, rows - chunk), pl.ds(0, half)], e_zs.at[0])
    await_bytes(err.at[:, pl.ds(0, half)], e_sib.at[0])
    await_bytes(errd.at[pl.ds(0, nt // 2), pl.ds(0, nz - 1)], d_zs.at[0])
    await_bytes(errd.at[pl.ds(0, nt // 2)], d_sib.at[0])
    await_bytes(lbuf.at[pl.ds(0, nt - 1)], l_sem.at[0])

    @pl.when(mine)
    def _():
        await_bytes(errd.at[pl.ds(0, nt - 1), 0], d_xs.at[0])


def on_device(nt, nf, ns, source_acts, target_acts, enc_weight, enc_bias, dec_weight, active_blocks):
    rows, width = source_acts.shape
    cols = enc_weight.shape[1]
    ny, nz = nt // NX, nf // PER_Z
    half, dblk, chunk = width // 2, width // nt, rows // nz
    enc_parts, n_tiles = 4, 4
    n_minus, n_plus = nz // 2, (nz - 1) // 2
    dma = lambda *shape: pltpu.SemaphoreType.DMA(shape)
    scratch = [
        pltpu.VMEM((rows, width), BF16),
        pltpu.VMEM((width, cols), BF16),
        pltpu.VMEM((cols, width), BF16),
        pltpu.VMEM((chunk, half), BF16),
        pltpu.VMEM((rows, cols), F32),
        pltpu.VMEM((rows, cols), F32),
        pltpu.VMEM((nt, rows, dblk), BF16),
        pltpu.VMEM((nt, rows, cols), BF16),
        pltpu.VMEM((nt, rows, cols), BF16),
        pltpu.VMEM((rows, width), BF16),
        pltpu.VMEM((nt, nz, chunk, dblk), BF16),
        pltpu.VMEM((rows, half), F32),
        pltpu.VMEM((rows, half), BF16),
        pltpu.VMEM((rows, half), BF16),
        pltpu.VMEM((nz - 1, ns, chunk, half // ns), BF16),
        pltpu.VMEM((nz - 1, ns, chunk, half // ns), BF16),
        pltpu.VMEM((ns, chunk, half // ns), BF16),
        pltpu.VMEM((ns, chunk, half // ns), BF16),
        pltpu.VMEM((nt, 8, 128), F32),
        dma(4), dma(enc_parts), dma(2), dma(2),
        dma(1), dma(ny), dma(ny), dma(ny), dma(ny),
        dma(1), dma(ny), dma(ny), dma(ny), dma(ny),
        dma(1), dma(n_tiles),
        dma(1), dma(nz - 1, ns), dma(1), dma(ns),
        dma(1), dma(n_minus), dma(max(n_plus, 1)), dma(3),
        dma(2), dma(1), dma(n_minus), dma(max(n_plus, 1)), dma(2),
        dma(2),
    ]
    vmem = pl.BlockSpec(memory_space=pltpu.VMEM)
    hbm = pl.BlockSpec(memory_space=pl.ANY)
    grad_encoder, grad_decoder, loss = pl.pallas_call(
        functools.partial(kernel, (nt, ny, nz, rows, width, cols, ns)),
        out_shape=(
            jax.ShapeDtypeStruct((dblk, cols), F32),
            jax.ShapeDtypeStruct((cols, dblk), F32),
            jax.ShapeDtypeStruct((1, 1), F32),
        ),
        in_specs=[hbm, hbm, hbm, vmem, hbm, vmem],
        out_specs=(vmem, vmem, pl.BlockSpec(memory_space=pltpu.SMEM)),
        scratch_shapes=scratch,
        compiler_params=pltpu.CompilerParams(
            collective_id=0, has_side_effects=True, vmem_limit_bytes=48 * 1024 * 1024
        ),
        name="step",
    )(source_acts, target_acts, enc_weight, enc_bias.reshape(1, cols), dec_weight, active_blocks)
    return grad_encoder, grad_decoder, loss.reshape(())


def solution(mesh):
    placed = (
        P("tok", None),
        P("tok", None),
        P(None, "feat"),
        P("feat"),
        P("feat", None),
        P("tok", None),
    )
    return jax.shard_map(
        functools.partial(on_device, mesh.shape["tok"], mesh.shape["feat"], 2),
        mesh=mesh,
        in_specs=placed,
        out_specs=(P("tok", "feat"), P("feat", "tok"), P()),
        check_vma=False,
    )
```

time: 765 us -> 114 us (0.15)
  waiting for transfers between devices: 677 us -> 0 us
  Pallas kernels: 0 us -> 104 us
  blocking collectives: 34.8 us -> 0 us
  matrix products: 19.9 us -> 0 us
  between operations: 15.6 us -> 2.38 us
    psum x1 -> x0, waiting for transfers between devices: 531 us -> none  [on_device(): recon = lax.psum(partial_rec, 'feat')]
    reduce_scatter x2 -> x0, waiting for transfers between devices: 145 us -> none  [the longest x1 101 us: on_device(): lax.psum_scatter(enc_term.astype(jnp.bfloat16), 'tok', scatter_dimension=...]
    pallas_call x0 -> x1, Pallas kernels: none -> 104 us  [on_device(): pl.pallas_call(functools.partial(kernel, (nt, ny, nz, rows, width, cols,...]
    psum x1 -> x0, blocking collectives: 34.8 us -> none  [on_device(): lax.psum(jnp.sum(errors * errors), 'tok') / (total_rows * width)]
    dot_general x4 -> x0, matrix products: 19.9 us -> none  [the longest x1 7.53 us: on_device(): lax.dot_general(source_acts, grad_pre, (((0,), (0,)), ((), ())), preferre...]
  transfers between devices with their start and end apart: 3 -> 0, of which waited for: 3 -> 0; matrix products, arithmetic and copies ran while one was open for 2% -> 0% of each run, Pallas kernels for 0% -> 0%
where the time goes in v1:
time: 114 us; the launch traced here: 112 us
  Pallas kernels  104 us (91%)
  local copies, waits for them, and re-layouts  5.67 us (5%)
  between operations  2.38 us (2%)
    pallas_call x1, Pallas kernels, on_device(): pl.pallas_call(functools.partial(kernel, (nt, ny, nz, rows, width, cols,...  104 us
    unnamed x8, local copies, waits for them, and re-layouts  4.99 us

profile of v1, /device:TPU:1, one launch (start us, length us, event | category | flops | bytes accessed | tf_op | source)
XLA Modules:
  0.0 112.0 jit_solution(11949338180213458549)
XLA Ops:
  0.6 0.7 reshape.12.bias_ref
  1.3 0.0 copy-start
  1.3 1.4 %copy-done = bf16[192,4096]{1,0:T(8,128)(2,1)S(1)} copy-done((bf16[192,4096]{1,0:T(8,128)(2,1)S(1)}, bf16[192,4096]{1,0:T(8,128)(2,1)}, u32[]{:S(2)}) %copy-start) | copy-done | bytes 1572888
  2.7 0.0 copy-start.1
  2.7 1.4 %copy-done.1 = bf16[192,4096]{1,0:T(8,128)(2,1)S(1)} copy-done((bf16[192,4096]{1,0:T(8,128)(2,1)S(1)}, bf16[192,4096]{1,0:T(8,128)(2,1)}, u32[]{:S(2)}) %copy-start.1) | copy-done | bytes 1572888
  4.1 0.0 copy-start.2
  4.1 0.7 copy-done.2
  4.8 104.0 %step.1 = (f32[256,384]{1,0:T(8,128)S(1)}, f32[384,256]{1,0:T(8,128)S(1)}, f32[1,1]{1,0:T(1,128)}) custom-call(bf16[192,4096]{1,0:T(8,128)(2,1)S(1)} %copy-done, bf16[192,4096]{1,0:T(8,128)(2,1)S(1)} %copy-done.1, bf16[4096,384]{1,0:T(8,128)(2,1)} %enc_hbm.1, f32[1,384]{1,0:T(1,128)S(1)} %reshape.12.bias_ref, bf16[384,4096]{1,0:T(8,128)(2,1)} %dec_hbm.1, ...), custom_call_target="tpu_custom_call" | custom-call | tf_op jit(solution)/shard_map/step/pallas_call | solution.py:377
  108.8 0.7 copy.12
  109.5 0.7 copy.13
Async XLA Ops:
  1.3 1.4 %copy-start = (bf16[192,4096]{1,0:T(8,128)(2,1)S(1)}, bf16[192,4096]{1,0:T(8,128)(2,1)}, u32[]{:S(2)}) copy-start(bf16[192,4096]{1,0:T(8,128)(2,1)} %src_hbm.1) | copy-start | bytes 4718596
  2.7 1.4 %copy-start.1 = (bf16[192,4096]{1,0:T(8,128)(2,1)S(1)}, bf16[192,4096]{1,0:T(8,128)(2,1)}, u32[]{:S(2)}) copy-start(bf16[192,4096]{1,0:T(8,128)(2,1)} %tgt_hbm.1) | copy-start | bytes 4718596
  4.1 0.7 copy-start.2

commit v2 on v1

v2 whole, which is shorter than its diff:
```python
import functools
import math

import jax
import jax.numpy as jnp
from jax import lax
from jax.experimental import pallas as pl
from jax.experimental.pallas import tpu as pltpu
from jax.sharding import PartitionSpec as P

BLOCK = 128
TILE = 64
NX = 4
PER_Z = 4
MESH = pl.DeviceIdType.MESH
F32 = jnp.float32
BF16 = jnp.bfloat16


def remote(src, dst, send_sem, recv_sem, device):
    pltpu.make_async_remote_copy(
        src_ref=src, dst_ref=dst, send_sem=send_sem, recv_sem=recv_sem, device_id=device, device_id_type=MESH
    ).start()


def await_bytes(ref, sem):
    pltpu.make_async_copy(ref, ref, sem).wait()


def kernel(dims, src_hbm, tgt_hbm, enc_hbm, bias_hbm, dec_hbm, act_hbm, genc_ref, gdec_ref, loss_ref, *scratch):
    nt, ny, nz, rows, width, cols, ns, e_subs = dims
    (src_v, enc_v, dec_v, bias_ref, act_ref, tgt_v, acc, slope, srcd, fa, ga, err, errd, part, psend, precv, rsend, rrecv, ysend, yrecv, lbuf, lpart,
     load_sem, enc_sem, xs_sem, sf_sem, f_send, f_y, f_p, f_m, f_r, g_send, g_y, g_p, g_m, g_r, ps_send, ps_recv,
     rs_send, rs_recv, yh_send, yh_recv, e_zs, e_zp, e_zm, e_sib, d_xs, d_zs, d_zp, d_zm, d_sib, l_sem) = scratch
    half = width // 2
    dblk = width // nt
    chunk = rows // nz
    hrow = rows // 2
    sub_w = half // ns
    n_minus, n_plus = nz // 2, (nz - 1) // 2
    enc_parts = enc_sem.shape[0]
    kpart = width // enc_parts
    n_tiles = ps_recv.shape[0]
    tile_w = half // n_tiles

    t, f = lax.axis_index("tok"), lax.axis_index("feat")
    x, yl = t // ny, t % ny
    z, yh, c = f // PER_Z, (f // 2) % 2, f % 2

    def zmod(v):
        return lax.rem(v + nz, nz)

    def fid(zz, hh, cc):
        return (zz * 2 + hh) * 2 + cc

    def tid(xx, yy):
        return lax.rem(xx + NX, NX) * ny + lax.rem(yy + ny, ny)

    def rows_of(zz):
        return pl.ds(pl.multiple_of(zz * chunk, chunk), chunk)

    def dcols(tt):
        return pl.ds(pl.multiple_of(tt * dblk, dblk), dblk)

    z_up, z_down = (t, fid(zmod(z + 1), yh, c)), (t, fid(zmod(z - 1), yh, c))
    sibling, y_peer = (t, fid(z, yh, 1 - c)), (t, fid(z, 1 - yh, c))
    own_half = pl.ds(pl.multiple_of(hrow * c, hrow), hrow)
    sib_half = pl.ds(pl.multiple_of(hrow * (1 - c), hrow), hrow)
    my_cols = pl.ds(pl.multiple_of(half * c, half), half)
    my_groups = pl.ds(c * (nt // 2), nt // 2)

    def load_enc(k):
        part_rows = pl.ds(k * kpart, kpart)
        return pltpu.make_async_copy(enc_hbm.at[part_rows], enc_v.at[part_rows], enc_sem.at[k])

    loads = [
        pltpu.make_async_copy(src_hbm, src_v, load_sem.at[0]),
        pltpu.make_async_copy(dec_hbm, dec_v, load_sem.at[1]),
        pltpu.make_async_copy(tgt_hbm.at[rows_of(z), my_cols], tgt_v, load_sem.at[2]),
        pltpu.make_async_copy(src_hbm.at[own_half, dcols(t)], srcd.at[t, own_half], load_sem.at[3]),
        pltpu.make_async_copy(bias_hbm, bias_ref, load_sem.at[4]),
        pltpu.make_async_copy(act_hbm, act_ref, load_sem.at[5]),
    ]
    loads[0].start()
    for k in range(enc_parts):
        load_enc(k).start()
    for load in loads[1:]:
        load.start()

    barrier = pltpu.get_barrier_semaphore()
    for k in range(1, nt):
        pl.semaphore_signal(barrier, inc=1, device_id=(lax.rem(t + k, nt), f), device_id_type=MESH)
    for peer in (z_up, z_down, sibling, y_peer):
        pl.semaphore_signal(barrier, inc=1, device_id=peer, device_id_type=MESH)
    pl.semaphore_wait(barrier, nt - 1 + 4)

    for load in (loads[0], loads[4], loads[5]):
        load.wait()
    acc[...] = jnp.broadcast_to(bias_ref[...][None, :], acc.shape)
    for k in range(enc_parts):
        load_enc(k).wait()
        part_rows = pl.ds(k * kpart, kpart)
        acc[...] += jnp.dot(src_v[:, part_rows], enc_v[part_rows, :], preferred_element_type=F32)

    for tile in range(rows // TILE):
        listed = act_ref[tile : tile + 1, :]
        for blk in range(cols // BLOCK):
            block_id = f * (cols // BLOCK) + blk
            active = jnp.max(jnp.where(listed == block_id, 1.0, 0.0), axis=1, keepdims=True)
            at = (pl.ds(tile * TILE, TILE), pl.ds(blk * BLOCK, BLOCK))
            v = acc[at]
            cdf = 0.5 * (1.0 + lax.erf(v * math.sqrt(0.5)))
            pdf = jnp.exp(-0.5 * v * v) * (1.0 / math.sqrt(2.0 * math.pi))
            fa[t, at[0], at[1]] = (v * cdf * active).astype(BF16)
            slope[at] = (cdf + v * pdf) * active

    def gather_start(part, send, y_sem, p_sem, m_sem):
        for k in range(1, ny):
            remote(part(t), part(t), send, y_sem.at[k], (tid(x, yl + k), f))
        gather_x(part, send, p_sem, m_sem, 0)

    def gather_x(part, send, p_sem, m_sem, k):
        own = part(tid(x, yl - k))
        remote(own, own, send, p_sem.at[k], (tid(x + 1, yl), f))
        remote(own, own, send, m_sem.at[k], (tid(x - 1, yl), f))

    def gather_y(part, send, y_sem, p_sem, m_sem):
        for k in range(1, ny):
            await_bytes(part(tid(x, yl - k)), y_sem.at[k])
            gather_x(part, send, p_sem, m_sem, k)

    def gather_relay(part, send, p_sem, m_sem, r_sem):
        for k in range(ny):
            below, above = part(tid(x - 1, yl - k)), part(tid(x + 1, yl - k))
            if k < ny // 2:
                await_bytes(below, p_sem.at[k])
                remote(below, below, send, r_sem.at[k], (tid(x + 1, yl), f))
                await_bytes(above, m_sem.at[k])
            else:
                await_bytes(above, m_sem.at[k])
                remote(above, above, send, r_sem.at[k], (tid(x - 1, yl), f))
                await_bytes(below, p_sem.at[k])

    def gather_far(part, r_sem):
        for k in range(ny):
            await_bytes(part(tid(x + 2, yl - k)), r_sem.at[k])

    near = max(1, n_minus // 2)
    n_early = 2 * near + 1
    cuts = (pl.ds(0, n_early * chunk), pl.ds(n_early * chunk, rows - n_early * chunk))

    def features_of(g):
        return fa.at[g]

    def grads_of(h):
        return lambda g: ga.at[g, cuts[h]]

    gather_start(features_of, f_send.at[0], f_y, f_p, f_m)

    for k in range(1, nt):
        to = lax.rem(t + k, nt)
        remote(src_hbm.at[own_half, dcols(to)], srcd.at[t, own_half], xs_sem.at[0], xs_sem.at[1], (to, f))

    loads[1].wait()

    @pl.loop(0, n_tiles)
    def _(n):
        at = pl.ds(pl.multiple_of(n * tile_w, tile_w), tile_w)
        full = pl.ds(pl.multiple_of(half * (1 - c) + n * tile_w, tile_w), tile_w)
        psend[:, at] = jnp.dot(fa[t], dec_v[:, full], preferred_element_type=F32).astype(BF16)
        remote(psend.at[:, at], precv.at[:, at], ps_send.at[0], ps_recv.at[n], sibling)

    @pl.loop(0, n_tiles)
    def _(n):
        at = pl.ds(pl.multiple_of(n * tile_w, tile_w), tile_w)
        full = pl.ds(pl.multiple_of(half * c + n * tile_w, tile_w), tile_w)
        part[:, at] = jnp.dot(fa[t], dec_v[:, full], preferred_element_type=F32)

    @pl.loop(0, n_tiles)
    def _(n):
        at = pl.ds(pl.multiple_of(n * tile_w, tile_w), tile_w)
        await_bytes(precv.at[:, at], ps_recv.at[n])
        part[:, at] += precv[:, at].astype(F32)

    def rs_step(slot, prev, owner, sub, device):
        value = part[rows_of(owner), pl.ds(sub * sub_w, sub_w)]
        if prev is not None:
            await_bytes(rrecv.at[prev, sub], rs_recv.at[prev, sub])
            value = value + rrecv[prev, sub].astype(F32)
        rsend[slot, sub] = value.astype(BF16)
        remote(rsend.at[slot, sub], rrecv.at[slot, sub], rs_send.at[0], rs_recv.at[slot, sub], device)

    for s in range(n_minus):
        for sub in range(ns):
            rs_step(s, s - 1 if s else None, zmod(z - (n_minus - s)), sub, z_down)
            if s < n_plus:
                rs_step(n_minus + s, n_minus + s - 1 if s else None, zmod(z + (n_plus - s)), sub, z_up)
    for sub in range(ns):
        value = part[rows_of(z), pl.ds(sub * sub_w, sub_w)]
        for last in (n_minus - 1, n_minus + n_plus - 1):
            await_bytes(rrecv.at[last, sub], rs_recv.at[last, sub])
            value = value + rrecv[last, sub].astype(F32)
        ysend[sub] = value.astype(BF16)
        remote(ysend.at[sub], yrecv.at[sub], yh_send.at[0], yh_recv.at[sub], y_peer)

    own_rows = pl.ds(near * chunk, chunk)
    gather_y(features_of, f_send.at[0], f_y, f_p, f_m)
    for sub in range(ns):
        await_bytes(yrecv.at[sub], yh_recv.at[sub])
        recon = ysend[sub].astype(F32) + yrecv[sub].astype(F32)
        target = tgt_v[:, pl.ds(sub * sub_w, sub_w)] if sub else None
        if sub == 0:
            loads[2].wait()
            target = tgt_v[:, pl.ds(0, sub_w)]
        at = pl.ds(pl.multiple_of(half * c + sub * sub_w, sub_w), sub_w)
        err[own_rows, at] = (recon - target.astype(F32)).astype(BF16)

    def ring_start(piece_of, next_of, subs, send, p_sem, m_sem, sib_send, sib_recv):
        for sub in range(subs):
            piece = piece_of(0, sub)
            remote(piece, piece, sib_send, sib_recv, sibling)
            remote(piece, next_of(0, -1, sub), send, p_sem.at[0, sub], z_up)
            remote(piece, next_of(0, 1, sub), send, m_sem.at[0, sub], z_down)

    def ring_step(piece_of, next_of, subs, s, send, p_sem, m_sem, sib_send, sib_recv):
        arrived = []
        for sub in range(subs):
            for sem, sign, hops, device in ((p_sem, -1, n_minus, z_up), (m_sem, 1, n_plus, z_down)):
                if s <= hops:
                    piece = piece_of(sign * s, sub)
                    await_bytes(piece, sem.at[s - 1, sub])
                    if s < hops:
                        remote(piece, next_of(sign * s, sign, sub), send, sem.at[s, sub], device)
                    arrived.append(piece)
        for piece in arrived:
            remote(piece, piece, sib_send, sib_recv, sibling)

    err_w = half // e_subs

    def err_piece(hop, sub):
        at = pl.ds((near + hop) % nz * chunk, chunk)
        return err.at[at, pl.ds(pl.multiple_of(half * c + err_w * sub, err_w), err_w)]

    def err_next(hop, sign, sub):
        return err_piece(hop + sign, sub)

    def errd_piece(hop, sub):
        return errd.at[my_groups, zmod(z + hop)]

    def errd_next(hop, sign, sub):
        return errd_piece(hop, sub)

    e_ring = (e_zs.at[0], e_zp, e_zm, e_sib.at[0])
    d_ring = (d_zs.at[0], d_zp, d_zm, d_sib.at[0], d_sib.at[1])
    mine = t // (nt // 2) == c

    def errd_send():
        await_bytes(err.at[own_rows, my_cols], e_sib.at[1])

        @pl.when(mine)
        def _():
            for k in range(1, nt):
                to = lax.rem(t + k, nt)
                remote(err.at[own_rows, dcols(to)], errd.at[t, z], d_xs.at[0], d_xs.at[1], (to, f))
            errd[t, z] = err[own_rows, dcols(t)]

    def errd_start():
        @pl.when(mine)
        def _():
            await_bytes(errd.at[pl.ds(0, nt // 2 - 1), 0], d_xs.at[1])

        @pl.when(jnp.logical_not(mine))
        def _():
            await_bytes(errd.at[pl.ds(0, nt // 2), 0], d_xs.at[1])

        ring_start(errd_piece, errd_next, 1, *d_ring)

    def errd_step(s):
        ring_step(errd_piece, errd_next, 1, s, *d_ring)

    def rows_at(place):
        return rows_of(zmod(z + place - near))

    def back(h):
        acc[cuts[h], :] = jnp.zeros((cuts[h].size, cols), F32)

        @pl.loop(0, enc_parts)
        def _(k):
            at = pl.ds(pl.multiple_of(k * kpart, kpart), kpart)
            acc[cuts[h], :] += lax.dot_general(
                err[cuts[h], at], dec_v[:, at], (((1,), (1,)), ((), ())), preferred_element_type=F32
            )

        for place in range(cuts[h].start // chunk, (cuts[h].start + cuts[h].size) // chunk):
            at = pl.ds(place * chunk, chunk)
            ga[t, at, :] = (acc[at, :] * slope[rows_at(place), :]).astype(BF16)
        gather_start(grads_of(h), g_send.at[h], g_y.at[h], g_p.at[h], g_m.at[h])

    ring_start(err_piece, err_next, e_subs, *e_ring, e_sib.at[1])
    d_lag = near
    for s in range(1, n_minus + 1):
        ring_step(err_piece, err_next, e_subs, s, *e_ring, e_sib.at[2 if s <= near else 3])
        if s == 1:
            errd_send()
        if s == 2:
            loads[3].wait()
            await_bytes(srcd.at[pl.ds(0, nt - 1), pl.ds(0, hrow)], xs_sem.at[1])
            remote(srcd.at[:, own_half], srcd.at[:, own_half], sf_sem.at[0], sf_sem.at[1], sibling)
        if s == 3:
            gather_relay(features_of, f_send.at[0], f_p, f_m, f_r)
        if s == d_lag:
            errd_start()
        if s > d_lag:
            errd_step(s - d_lag)
        if s == near + 1:
            await_bytes(err.at[pl.ds(0, (n_early - 1) * chunk), pl.ds(0, half)], e_sib.at[2])
            back(0)
    await_bytes(err.at[pl.ds(0, rows - n_early * chunk), pl.ds(0, half)], e_sib.at[3])
    back(1)

    errd_step(n_minus - d_lag + 1)
    gather_y(grads_of(0), g_send.at[0], g_y.at[0], g_p.at[0], g_m.at[0])

    for place in range(nz):
        total = jnp.zeros((16, 128), F32)
        for r in range(chunk // 16):
            for k in range(width // 128):
                piece = err[pl.ds(place * chunk + r * 16, 16), pl.ds(k * 128, 128)].astype(F32)
                total = total + piece * piece
        lpart[zmod(z + place - near)] = total[:8] + total[8:]
    total = lpart[0]
    for k in range(1, nz):
        total = total + lpart[k]
    lbuf[t] = total
    for k in range(1, nt):
        remote(lbuf.at[t], lbuf.at[t], l_sem.at[0], l_sem.at[1], (lax.rem(t + k, nt), f))

    if n_minus - d_lag + 2 <= n_minus:
        errd_step(n_minus - d_lag + 2)
    gather_y(grads_of(1), g_send.at[1], g_y.at[1], g_p.at[1], g_m.at[1])
    gather_relay(grads_of(0), g_send.at[0], g_p.at[0], g_m.at[0], g_r.at[0])
    for s in range(n_minus - d_lag + 3, n_minus + 1):
        errd_step(s)

    across = (((0,), (0,)), ((), ()))
    genc_ref[...] = jnp.zeros_like(genc_ref)
    gdec_ref[...] = jnp.zeros_like(gdec_ref)

    def enc_groups(dx):
        @pl.loop(0, ny)
        def _(k):
            g = tid(x + dx, yl - k)
            source = jnp.concatenate([srcd[g, rows_at(place), :] for place in range(nz)], axis=0)
            genc_ref[...] += lax.dot_general(source, ga[g], across, preferred_element_type=F32)

    def dec_groups(first):
        @pl.loop(first, first + nt // 2)
        def _(g):
            gdec_ref[...] += lax.dot_general(fa[g], errd[g].reshape(rows, dblk), across, preferred_element_type=F32)

    await_bytes(srcd.at[:, sib_half], sf_sem.at[1])
    enc_groups(0)
    gather_relay(grads_of(1), g_send.at[1], g_p.at[1], g_m.at[1], g_r.at[1])
    gather_far(features_of, f_r)
    await_bytes(errd.at[pl.ds(0, nt // 2)], d_sib.at[1])
    dec_groups(0)
    dec_groups(nt // 2)
    enc_groups(1)
    enc_groups(-1)
    await_bytes(lbuf.at[pl.ds(0, nt - 1)], l_sem.at[1])
    sums = lbuf[0]
    for k in range(1, nt):
        sums = sums + lbuf[k]
    loss_ref[0, 0] = jnp.sum(sums) / (rows * nt * width)
    gather_far(grads_of(0), g_r.at[0])
    gather_far(grads_of(1), g_r.at[1])
    enc_groups(2)

    await_bytes(srcd.at[pl.ds(0, nt - 1), pl.ds(0, hrow)], xs_sem.at[0])
    await_bytes(srcd.at[:, own_half], sf_sem.at[0])
    await_bytes(fa.at[pl.ds(0, nt - 1)], f_send.at[0])
    for h in range(2):
        await_bytes(ga.at[pl.ds(0, nt - 1), cuts[h]], g_send.at[h])
    await_bytes(psend, ps_send.at[0])
    await_bytes(rsend, rs_send.at[0])
    await_bytes(ysend, yh_send.at[0])
    await_bytes(err.at[pl.ds(0, rows - chunk), pl.ds(0, half)], e_zs.at[0])
    await_bytes(err.at[:, pl.ds(0, half)], e_sib.at[0])
    await_bytes(errd.at[pl.ds(0, nt // 2), pl.ds(0, nz - 1)], d_zs.at[0])
    await_bytes(errd.at[pl.ds(0, nt // 2)], d_sib.at[0])
    await_bytes(lbuf.at[pl.ds(0, nt - 1)], l_sem.at[0])

    @pl.when(mine)
    def _():
        await_bytes(errd.at[pl.ds(0, nt - 1), 0], d_xs.at[0])


def on_device(nt, nf, ns, e_subs, source_acts, target_acts, enc_weight, enc_bias, dec_weight, active_blocks):
    rows, width = source_acts.shape
    cols = enc_weight.shape[1]
    ny, nz = nt // NX, nf // PER_Z
    half, dblk, chunk = width // 2, width // nt, rows // nz
    enc_parts, n_tiles = 4, 4
    n_minus, n_plus = nz // 2, (nz - 1) // 2
    dma = lambda *shape: pltpu.SemaphoreType.DMA(shape)
    scratch = [
        pltpu.VMEM((rows, width), BF16),
        pltpu.VMEM((width, cols), BF16),
        pltpu.VMEM((cols, width), BF16),
        pltpu.VMEM((cols,), F32),
        pltpu.VMEM(active_blocks.shape, jnp.int32),
        pltpu.VMEM((chunk, half), BF16),
        pltpu.VMEM((rows, cols), F32),
        pltpu.VMEM((rows, cols), F32),
        pltpu.VMEM((nt, rows, dblk), BF16),
        pltpu.VMEM((nt, rows, cols), BF16),
        pltpu.VMEM((nt, rows, cols), BF16),
        pltpu.VMEM((rows, width), BF16),
        pltpu.VMEM((nt, nz, chunk, dblk), BF16),
        pltpu.VMEM((rows, half), F32),
        pltpu.VMEM((rows, half), BF16),
        pltpu.VMEM((rows, half), BF16),
        pltpu.VMEM((nz - 1, ns, chunk, half // ns), BF16),
        pltpu.VMEM((nz - 1, ns, chunk, half // ns), BF16),
        pltpu.VMEM((ns, chunk, half // ns), BF16),
        pltpu.VMEM((ns, chunk, half // ns), BF16),
        pltpu.VMEM((nt, 8, 128), F32),
        pltpu.VMEM((nz, 8, 128), F32),
        dma(6), dma(enc_parts), dma(2), dma(2),
        dma(1), dma(ny), dma(ny), dma(ny), dma(ny),
        dma(2), dma(2, ny), dma(2, ny), dma(2, ny), dma(2, ny),
        dma(1), dma(n_tiles),
        dma(1), dma(nz - 1, ns), dma(1), dma(ns),
        dma(1), dma(n_minus, e_subs), dma(n_plus, e_subs), dma(4),
        dma(2), dma(1), dma(n_minus, 1), dma(n_plus, 1), dma(2),
        dma(2),
    ]
    vmem = pl.BlockSpec(memory_space=pltpu.VMEM)
    hbm = pl.BlockSpec(memory_space=pltpu.HBM)
    grad_encoder, grad_decoder, loss = pl.pallas_call(
        functools.partial(kernel, (nt, ny, nz, rows, width, cols, ns, e_subs)),
        out_shape=(
            jax.ShapeDtypeStruct((dblk, cols), F32),
            jax.ShapeDtypeStruct((cols, dblk), F32),
            jax.ShapeDtypeStruct((1, 1), F32),
        ),
        in_specs=[hbm] * 6,
        out_specs=(vmem, vmem, pl.BlockSpec(memory_space=pltpu.SMEM)),
        scratch_shapes=scratch,
        compiler_params=pltpu.CompilerParams(
            collective_id=0, has_side_effects=True, vmem_limit_bytes=60 * 1024 * 1024
        ),
        name="step",
    )(source_acts, target_acts, enc_weight, enc_bias, dec_weight, active_blocks)
    return grad_encoder, grad_decoder, loss.reshape(())


def solution(mesh):
    placed = (
        P("tok", None),
        P("tok", None),
        P(None, "feat"),
        P("feat"),
        P("feat", None),
        P("tok", None),
    )
    return jax.shard_map(
        functools.partial(on_device, mesh.shape["tok"], mesh.shape["feat"], 2, 2),
        mesh=mesh,
        in_specs=placed,
        out_specs=(P("tok", "feat"), P("feat", "tok"), P()),
        check_vma=False,
    )
```

time: 114 us -> 103 us (0.904); the launches traced: 112 us -> 103 us
  Pallas kernels: 104 us -> 96.7 us
  local copies, waits for them, and re-layouts: 5.67 us -> 3.53 us
    pallas_call x1, Pallas kernels: 104 us -> 96.7 us  [on_device(): pl.pallas_call(functools.partial(kernel, (nt, ny, nz, rows, width, cols,...]
    unnamed x8 -> x2, local copies, waits for them, and re-layouts: 4.99 us -> 3.53 us
where the time goes in v2:
time: 103 us
  Pallas kernels  96.7 us (94%)
  local copies, waits for them, and re-layouts  3.53 us (3%)
  between operations  2.32 us (2%)
    pallas_call x1, Pallas kernels, on_device(): pl.pallas_call(functools.partial(kernel, (nt, ny, nz, rows, width, cols,...  96.7 us
    unnamed x2, local copies, waits for them, and re-layouts  3.53 us

profile of v2, /device:TPU:1, one launch (start us, length us, event | category | flops | bytes accessed | tf_op | source)
XLA Modules:
  0.0 102.5 jit_solution(6217995024162886730)
XLA Ops:
  0.6 96.7 %step.1 = (f32[256,384]{1,0:T(8,128)}, f32[384,256]{1,0:T(8,128)}, f32[1,1]{1,0:T(1,128)}) custom-call(bf16[192,4096]{1,0:T(8,128)(2,1)} %src_hbm.1, bf16[192,4096]{1,0:T(8,128)(2,1)} %tgt_hbm.1, bf16[4096,384]{1,0:T(8,128)(2,1)} %enc_hbm.1, f32[384]{0:T(512)} %bias_hbm.1, bf16[384,4096]{1,0:T(8,128)(2,1)} %dec_hbm.1, s32[3,48]{1,0:T(4,128)} %act_hbm.1), custom_call_target="tpu_custom_call" | custom-call | tf_op jit(solution)/shard_map/step/pallas_call | solution.py:440
  97.3 1.8 %copy.12 = f32[256,384]{1,0:T(8,128)} copy(f32[256,384]{1,0:T(8,128)} %get-tuple-element.12) | data formatting | bytes 786432
  99.1 1.8 %copy.13 = f32[384,256]{1,0:T(8,128)} copy(f32[384,256]{1,0:T(8,128)} %get-tuple-element.13) | data formatting | bytes 786432

commit v3 on v2

--- a/solution.py
+++ b/solution.py
@@ -30,7 +30,7 @@
 def kernel(dims, src_hbm, tgt_hbm, enc_hbm, bias_hbm, dec_hbm, act_hbm, genc_ref, gdec_ref, loss_ref, *scratch):
     nt, ny, nz, rows, width, cols, ns, e_subs = dims
     (src_v, enc_v, dec_v, bias_ref, act_ref, tgt_v, acc, slope, srcd, fa, ga, err, errd, part, psend, precv, rsend, rrecv, ysend, yrecv, lbuf, lpart,
-     load_sem, enc_sem, xs_sem, sf_sem, f_send, f_y, f_p, f_m, f_r, g_send, g_y, g_p, g_m, g_r, ps_send, ps_recv,
+     load_sem, enc_sem, xs_sem, sf_sem, f_send, f_y, f_p, f_m, f_r, g_send, g_y, g_p, g_m, g_r, g_all, ps_send, ps_recv,
      rs_send, rs_recv, yh_send, yh_recv, e_zs, e_zp, e_zm, e_sib, d_xs, d_zs, d_zp, d_zm, d_sib, l_sem) = scratch
     half = width // 2
     dblk = width // nt
@@ -145,9 +145,18 @@
         for k in range(ny):
             await_bytes(part(tid(x + 2, yl - k)), r_sem.at[k])
 
-    near = max(1, n_minus // 2)
-    n_early = 2 * near + 1
-    cuts = (pl.ds(0, n_early * chunk), pl.ds(n_early * chunk, rows - n_early * chunk))
+    hops_of = (n_minus // 3, 2 * n_minus // 3, n_minus)
+    ends = [min(2 * hops + 1, nz) for hops in hops_of]
+    starts = [0] + ends[:2]
+    cuts = [pl.ds(a * chunk, (b - a) * chunk) for a, b in zip(starts, ends)]
+    last = len(cuts) - 1
+
+    def place_of(hop):
+        return 2 * hop if hop >= 0 else -2 * hop - 1
+
+    def hop_at(place):
+        return -(place + 1) // 2 if place % 2 else place // 2
+
 
     def features_of(g):
         return fa.at[g]
@@ -197,13 +206,13 @@
                 rs_step(n_minus + s, n_minus + s - 1 if s else None, zmod(z + (n_plus - s)), sub, z_up)
     for sub in range(ns):
         value = part[rows_of(z), pl.ds(sub * sub_w, sub_w)]
-        for last in (n_minus - 1, n_minus + n_plus - 1):
-            await_bytes(rrecv.at[last, sub], rs_recv.at[last, sub])
-            value = value + rrecv[last, sub].astype(F32)
+        for slot in (n_minus - 1, n_minus + n_plus - 1):
+            await_bytes(rrecv.at[slot, sub], rs_recv.at[slot, sub])
+            value = value + rrecv[slot, sub].astype(F32)
         ysend[sub] = value.astype(BF16)
         remote(ysend.at[sub], yrecv.at[sub], yh_send.at[0], yh_recv.at[sub], y_peer)
 
-    own_rows = pl.ds(near * chunk, chunk)
+    own_rows = pl.ds(0, chunk)
     gather_y(features_of, f_send.at[0], f_y, f_p, f_m)
     for sub in range(ns):
         await_bytes(yrecv.at[sub], yh_recv.at[sub])
@@ -238,7 +247,7 @@
     err_w = half // e_subs
 
     def err_piece(hop, sub):
-        at = pl.ds((near + hop) % nz * chunk, chunk)
+        at = pl.ds(place_of(hop) * chunk, chunk)
         return err.at[at, pl.ds(pl.multiple_of(half * c + err_w * sub, err_w), err_w)]
 
     def err_next(hop, sign, sub):
@@ -276,10 +285,16 @@
         ring_start(errd_piece, errd_next, 1, *d_ring)
 
     def errd_step(s):
-        ring_step(errd_piece, errd_next, 1, s, *d_ring)
+        ring_step(errd_piece, errd_next, 1, s, *d_ring[:4], d_sib.at[1 if s <= d_first else 2])
 
     def rows_at(place):
-        return rows_of(zmod(z + place - near))
+        return rows_of(zmod(z + hop_at(place)))
+
+    def g_sems(h):
+        return g_send.at[h], g_y.at[h], g_p.at[h], g_m.at[h]
+
+    def g_relay(h):
+        gather_relay(grads_of(h), g_send.at[h], g_p.at[h], g_m.at[h], g_r.at[h])
 
     def back(h):
         acc[cuts[h], :] = jnp.zeros((cuts[h].size, cols), F32)
@@ -291,80 +306,108 @@
                 err[cuts[h], at], dec_v[:, at], (((1,), (1,)), ((), ())), preferred_element_type=F32
             )
 
-        for place in range(cuts[h].start // chunk, (cuts[h].start + cuts[h].size) // chunk):
+        for place in range(starts[h], ends[h]):
             at = pl.ds(place * chunk, chunk)
             ga[t, at, :] = (acc[at, :] * slope[rows_at(place), :]).astype(BF16)
-        gather_start(grads_of(h), g_send.at[h], g_y.at[h], g_p.at[h], g_m.at[h])
+        if h < last:
+            gather_start(grads_of(h), *g_sems(h))
+        else:
+            for k in range(1, nt):
+                remote(ga.at[t, cuts[h]], ga.at[t, cuts[h]], g_all.at[0], g_all.at[1], (lax.rem(t + k, nt), f))
 
     ring_start(err_piece, err_next, e_subs, *e_ring, e_sib.at[1])
-    d_lag = near
-    for s in range(1, n_minus + 1):
-        ring_step(err_piece, err_next, e_subs, s, *e_ring, e_sib.at[2 if s <= near else 3])
-        if s == 1:
-            errd_send()
-        if s == 2:
-            loads[3].wait()
-            await_bytes(srcd.at[pl.ds(0, nt - 1), pl.ds(0, hrow)], xs_sem.at[1])
-            remote(srcd.at[:, own_half], srcd.at[:, own_half], sf_sem.at[0], sf_sem.at[1], sibling)
-        if s == 3:
-            gather_relay(features_of, f_send.at[0], f_p, f_m, f_r)
-        if s == d_lag:
-            errd_start()
-        if s > d_lag:
-            errd_step(s - d_lag)
-        if s == near + 1:
-            await_bytes(err.at[pl.ds(0, (n_early - 1) * chunk), pl.ds(0, half)], e_sib.at[2])
-            back(0)
-    await_bytes(err.at[pl.ds(0, rows - n_early * chunk), pl.ds(0, half)], e_sib.at[3])
-    back(1)
-
-    errd_step(n_minus - d_lag + 1)
-    gather_y(grads_of(0), g_send.at[0], g_y.at[0], g_p.at[0], g_m.at[0])
-
-    for place in range(nz):
-        total = jnp.zeros((16, 128), F32)
-        for r in range(chunk // 16):
-            for k in range(width // 128):
-                piece = err[pl.ds(place * chunk + r * 16, 16), pl.ds(k * 128, 128)].astype(F32)
-                total = total + piece * piece
-        lpart[zmod(z + place - near)] = total[:8] + total[8:]
-    total = lpart[0]
-    for k in range(1, nz):
-        total = total + lpart[k]
-    lbuf[t] = total
-    for k in range(1, nt):
-        remote(lbuf.at[t], lbuf.at[t], l_sem.at[0], l_sem.at[1], (lax.rem(t + k, nt), f))
-
-    if n_minus - d_lag + 2 <= n_minus:
-        errd_step(n_minus - d_lag + 2)
-    gather_y(grads_of(1), g_send.at[1], g_y.at[1], g_p.at[1], g_m.at[1])
-    gather_relay(grads_of(0), g_send.at[0], g_p.at[0], g_m.at[0], g_r.at[0])
-    for s in range(n_minus - d_lag + 3, n_minus + 1):
-        errd_step(s)
-
     across = (((0,), (0,)), ((), ()))
     genc_ref[...] = jnp.zeros_like(genc_ref)
     gdec_ref[...] = jnp.zeros_like(gdec_ref)
+
+    def dec_terms(hop):
+        zz = zmod(z + hop)
+        feats = jnp.concatenate([fa[g, rows_of(zz), :] for g in range(nt)], axis=0)
+        errs = jnp.concatenate([errd[g, zz] for g in range(nt)], axis=0)
+        gdec_ref[...] += lax.dot_general(feats, errs, across, preferred_element_type=F32)
+
+    def dec_hops(first, stop):
+        for hop in range(first, stop):
+            for signed in ((0,) if hop == 0 else (-hop, hop) if hop <= n_plus else (-hop,)):
+                dec_terms(signed)
 
     def enc_groups(dx):
         @pl.loop(0, ny)
         def _(k):
             g = tid(x + dx, yl - k)
-            source = jnp.concatenate([srcd[g, rows_at(place), :] for place in range(nz)], axis=0)
-            genc_ref[...] += lax.dot_general(source, ga[g], across, preferred_element_type=F32)
-
-    def dec_groups(first):
-        @pl.loop(first, first + nt // 2)
-        def _(g):
-            gdec_ref[...] += lax.dot_general(fa[g], errd[g].reshape(rows, dblk), across, preferred_element_type=F32)
-
+            source = jnp.concatenate([srcd[g, rows_at(place), :] for place in range(starts[last])], axis=0)
+            grads = ga[g, pl.ds(0, starts[last] * chunk), :]
+            genc_ref[...] += lax.dot_general(source, grads, across, preferred_element_type=F32)
+
+    def enc_late():
+        @pl.loop(0, nt // 4)
+        def _(n):
+            groups = [n * 4 + k for k in range(4)]
+            source = jnp.concatenate(
+                [srcd[g, rows_at(place), :] for g in groups for place in range(starts[last], nz)], axis=0
+            )
+            grads = jnp.concatenate([ga[g, cuts[last], :] for g in groups], axis=0)
+            genc_ref[...] += lax.dot_general(source, grads, across, preferred_element_type=F32)
+
+    def loss_rows(h):
+        for place in range(starts[h], ends[h]):
+            total = jnp.zeros((16, 128), F32)
+            for r in range(chunk // 16):
+                for k in range(width // 128):
+                    piece = err[pl.ds(place * chunk + r * 16, 16), pl.ds(k * 128, 128)].astype(F32)
+                    total = total + piece * piece
+            lpart[zmod(z + hop_at(place))] = total[:8] + total[8:]
+
+    def loss_send():
+        total = lpart[0]
+        for k in range(1, nz):
+            total = total + lpart[k]
+        lbuf[t] = total
+        for k in range(1, nt):
+            remote(lbuf.at[t], lbuf.at[t], l_sem.at[0], l_sem.at[1], (lax.rem(t + k, nt), f))
+
+    def sibling_errors(h):
+        first = max(starts[h], 1)
+        await_bytes(err.at[pl.ds(0, (ends[h] - first) * chunk), pl.ds(0, half)], e_sib.at[2 + h])
+
+    d_lag = 3
+    d_first = n_minus - d_lag
+    for s in range(1, n_minus + 1):
+        h = [s <= hops for hops in hops_of].index(True)
+        ring_step(err_piece, err_next, e_subs, s, *e_ring, e_sib.at[2 + h])
+        if s > d_lag:
+            errd_step(s - d_lag)
+        if s == 1:
+            errd_send()
+        if s == n_minus:
+            gather_y(grads_of(1), *g_sems(1))
+            g_relay(0)
+        if s == hops_of[h]:
+            sibling_errors(h)
+            back(h)
+        if s == d_lag - 1:
+            errd_start()
+        if s in (3, 5):
+            loss_rows(h - 1)
+        if s == 3:
+            gather_relay(features_of, f_send.at[0], f_p, f_m, f_r)
+        if s == 5:
+            gather_y(grads_of(0), *g_sems(0))
+            loads[3].wait()
+            await_bytes(srcd.at[pl.ds(0, nt - 1), pl.ds(0, hrow)], xs_sem.at[1])
+            remote(srcd.at[:, own_half], srcd.at[:, own_half], sf_sem.at[0], sf_sem.at[1], sibling)
+
+    errd_step(d_first + 1)
+    loss_rows(last)
+    loss_send()
+    gather_far(features_of, f_r)
+    await_bytes(errd.at[pl.ds(0, nt // 2), pl.ds(0, 2 * d_first + 1)], d_sib.at[1])
+    dec_hops(0, d_first + 1)
+    errd_step(d_first + 2)
     await_bytes(srcd.at[:, sib_half], sf_sem.at[1])
     enc_groups(0)
-    gather_relay(grads_of(1), g_send.at[1], g_p.at[1], g_m.at[1], g_r.at[1])
-    gather_far(features_of, f_r)
-    await_bytes(errd.at[pl.ds(0, nt // 2)], d_sib.at[1])
-    dec_groups(0)
-    dec_groups(nt // 2)
+    g_relay(1)
+    errd_step(d_first + 3)
     enc_groups(1)
     enc_groups(-1)
     await_bytes(lbuf.at[pl.ds(0, nt - 1)], l_sem.at[1])
@@ -372,15 +415,20 @@
     for k in range(1, nt):
         sums = sums + lbuf[k]
     loss_ref[0, 0] = jnp.sum(sums) / (rows * nt * width)
-    gather_far(grads_of(0), g_r.at[0])
-    gather_far(grads_of(1), g_r.at[1])
+    await_bytes(errd.at[pl.ds(0, nt // 2), pl.ds(0, nz - 2 * d_first - 1)], d_sib.at[2])
+    dec_hops(d_first + 1, n_minus + 1)
+    for h in range(last):
+        gather_far(grads_of(h), g_r.at[h])
     enc_groups(2)
+    await_bytes(ga.at[pl.ds(0, nt - 1), cuts[last]], g_all.at[1])
+    enc_late()
 
     await_bytes(srcd.at[pl.ds(0, nt - 1), pl.ds(0, hrow)], xs_sem.at[0])
     await_bytes(srcd.at[:, own_half], sf_sem.at[0])
     await_bytes(fa.at[pl.ds(0, nt - 1)], f_send.at[0])
-    for h in range(2):
+    for h in range(last):
         await_bytes(ga.at[pl.ds(0, nt - 1), cuts[h]], g_send.at[h])
+    await_bytes(ga.at[pl.ds(0, nt - 1), cuts[last]], g_all.at[0])
     await_bytes(psend, ps_send.at[0])
     await_bytes(rsend, rs_send.at[0])
     await_bytes(ysend, yh_send.at[0])
@@ -428,11 +476,11 @@
         pltpu.VMEM((nz, 8, 128), F32),
         dma(6), dma(enc_parts), dma(2), dma(2),
         dma(1), dma(ny), dma(ny), dma(ny), dma(ny),
-        dma(2), dma(2, ny), dma(2, ny), dma(2, ny), dma(2, ny),
+        dma(2), dma(2, ny), dma(2, ny), dma(2, ny), dma(2, ny), dma(2),
         dma(1), dma(n_tiles),
         dma(1), dma(nz - 1, ns), dma(1), dma(ns),
-        dma(1), dma(n_minus, e_subs), dma(n_plus, e_subs), dma(4),
-        dma(2), dma(1), dma(n_minus, 1), dma(n_plus, 1), dma(2),
+        dma(1), dma(n_minus, e_subs), dma(n_plus, e_subs), dma(5),
+        dma(2), dma(1), dma(n_minus, 1), dma(n_plus, 1), dma(3),
         dma(2),
     ]
     vmem = pl.BlockSpec(memory_space=pltpu.VMEM)

time: 103 us -> 101 us (0.981); the launches traced: 103 us -> 99.4 us
  Pallas kernels: 96.7 us -> 93.5 us
    pallas_call x1, Pallas kernels: 96.7 us -> 93.5 us  [on_device(): pl.pallas_call(functools.partial(kernel, (nt, ny, nz, rows, width, cols,...]
where the time goes in v3:
time: 101 us; the launch traced here: 99.4 us
  Pallas kernels  93.5 us (93%)
  local copies, waits for them, and re-layouts  3.53 us (3%)
  between operations  2.32 us (2%)
    pallas_call x1, Pallas kernels, on_device(): pl.pallas_call(functools.partial(kernel, (nt, ny, nz, rows, width, cols,...  93.5 us
    unnamed x2, local copies, waits for them, and re-layouts  3.53 us

profile of v3, /device:TPU:1, one launch (start us, length us, event | category | flops | bytes accessed | tf_op | source)
XLA Modules:
  0.0 99.4 jit_solution(16869002699964780505)
XLA Ops:
  0.6 93.5 %step.1 = (f32[256,384]{1,0:T(8,128)}, f32[384,256]{1,0:T(8,128)}, f32[1,1]{1,0:T(1,128)}) custom-call(bf16[192,4096]{1,0:T(8,128)(2,1)} %src_hbm.1, bf16[192,4096]{1,0:T(8,128)(2,1)} %tgt_hbm.1, bf16[4096,384]{1,0:T(8,128)(2,1)} %enc_hbm.1, f32[384]{0:T(512)} %bias_hbm.1, bf16[384,4096]{1,0:T(8,128)(2,1)} %dec_hbm.1, s32[3,48]{1,0:T(4,128)} %act_hbm.1), custom_call_target="tpu_custom_call" | custom-call | tf_op jit(solution)/shard_map/step/pallas_call | solution.py:488
  94.2 1.8 %copy.12 = f32[256,384]{1,0:T(8,128)} copy(f32[256,384]{1,0:T(8,128)} %get-tuple-element.12) | data formatting | bytes 786432
  96.0 1.8 %copy.13 = f32[384,256]{1,0:T(8,128)} copy(f32[384,256]{1,0:T(8,128)} %get-tuple-element.13) | data formatting | bytes 786432

commit v4 on v3

--- a/solution.py
+++ b/solution.py
@@ -92,7 +92,6 @@
         pl.semaphore_signal(barrier, inc=1, device_id=(lax.rem(t + k, nt), f), device_id_type=MESH)
     for peer in (z_up, z_down, sibling, y_peer):
         pl.semaphore_signal(barrier, inc=1, device_id=peer, device_id_type=MESH)
-    pl.semaphore_wait(barrier, nt - 1 + 4)
 
     for load in (loads[0], loads[4], loads[5]):
         load.wait()
@@ -164,11 +163,8 @@
     def grads_of(h):
         return lambda g: ga.at[g, cuts[h]]
 
+    pl.semaphore_wait(barrier, nt - 1 + 4)
     gather_start(features_of, f_send.at[0], f_y, f_p, f_m)
-
-    for k in range(1, nt):
-        to = lax.rem(t + k, nt)
-        remote(src_hbm.at[own_half, dcols(to)], srcd.at[t, own_half], xs_sem.at[0], xs_sem.at[1], (to, f))
 
     loads[1].wait()
 
@@ -204,6 +200,10 @@
             rs_step(s, s - 1 if s else None, zmod(z - (n_minus - s)), sub, z_down)
             if s < n_plus:
                 rs_step(n_minus + s, n_minus + s - 1 if s else None, zmod(z + (n_plus - s)), sub, z_up)
+        if s == 0:
+            for k in range(1, nt):
+                to = lax.rem(t + k, nt)
+                remote(src_hbm.at[own_half, dcols(to)], srcd.at[t, own_half], xs_sem.at[0], xs_sem.at[1], (to, f))
     for sub in range(ns):
         value = part[rows_of(z), pl.ds(sub * sub_w, sub_w)]
         for slot in (n_minus - 1, n_minus + n_plus - 1):

time: 101 us -> 100 us (0.990); the launches traced: 99.4 us -> 100 us
  no operation moved by 1% of the time
where the time goes in v4:
time: 100 us
  Pallas kernels  94.4 us (94%)
  local copies, waits for them, and re-layouts  3.53 us (4%)
  between operations  2.32 us (2%)
    pallas_call x1, Pallas kernels, on_device(): pl.pallas_call(functools.partial(kernel, (nt, ny, nz, rows, width, cols,...  94.4 us
    unnamed x2, local copies, waits for them, and re-layouts  3.53 us

profile of v4, /device:TPU:1, one launch (start us, length us, event | category | flops | bytes accessed | tf_op | source)
XLA Modules:
  0.0 100.2 jit_solution(10719556749893181448)
XLA Ops:
  0.6 94.4 %step.1 = (f32[256,384]{1,0:T(8,128)}, f32[384,256]{1,0:T(8,128)}, f32[1,1]{1,0:T(1,128)}) custom-call(bf16[192,4096]{1,0:T(8,128)(2,1)} %src_hbm.1, bf16[192,4096]{1,0:T(8,128)(2,1)} %tgt_hbm.1, bf16[4096,384]{1,0:T(8,128)(2,1)} %enc_hbm.1, f32[384]{0:T(512)} %bias_hbm.1, bf16[384,4096]{1,0:T(8,128)(2,1)} %dec_hbm.1, s32[3,48]{1,0:T(4,128)} %act_hbm.1), custom_call_target="tpu_custom_call" | custom-call | tf_op jit(solution)/shard_map/step/pallas_call | solution.py:488
  95.0 1.8 %copy.12 = f32[256,384]{1,0:T(8,128)} copy(f32[256,384]{1,0:T(8,128)} %get-tuple-element.12) | data formatting | bytes 786432
  96.8 1.8 %copy.13 = f32[384,256]{1,0:T(8,128)} copy(f32[384,256]{1,0:T(8,128)} %get-tuple-element.13) | data formatting | bytes 786432
